TPU v7x, 256 devices: a whole 4x4x8 slice. The times are simulated.
256 devices in a mesh: row: 16 (over z, core), col: 4 (over y), rep: 4 (over x).
Axes of the slice: x: 4, y: 4, z: 8, core: 2. Of those that a mesh axis runs over, the one named last changes fastest.
Arguments:
- density: bfloat16 [8192, 8192], P('row', 'col'), may hold values from -1.5 to 1.75, as said below
- pattern_density: int32 [256, 256], P('row', 'col'), may hold values 0 or 1
- pattern_square: int32 [256, 256], P('row', 'col'), may hold values 0 or 1
- pattern_cube: int32 [256, 256], P('row', 'col'), may hold values 0 or 1
Outputs:
- purified: bfloat16 [8192, 8192], P('row', ('col', 'rep'))
Inputs may be any that keep to these rules, and one draw needn't show every extreme that they name: `density`: symmetric.
All inputs are finite; a program needn't handle non-finite values. No bound on the sum of `pattern_density` or of `pattern_square` or of `pattern_cube` on one device may be relied on, other than what follows from the above.
Results may differ from a plain program's by a relative error of at most 0.0054.
Values may be sent and summed in bfloat16 or wider, within the bound.
No kernel may reach another device: no remote copies, remote signals or barrier semaphores. Data moves between devices by JAX's collectives and lax.ppermute only.
A program may use at most 64 MiB of HBM per device.

v0:
```python
import jax
import jax.numpy as jnp
from jax import lax
from jax.sharding import PartitionSpec as P

BLK = 32


def spread(pattern, block_width):
    blocks_down, blocks_across = pattern.shape
    wide = jnp.broadcast_to(
        pattern[:, None, :, None] > 0, (blocks_down, block_width, blocks_across, block_width)
    )
    return wide.reshape(blocks_down * block_width, blocks_across * block_width)


def column_share(matrix, rep_depth, rep_layer, block_width):
    tile_rows, tile_width = matrix.shape
    shaped = matrix.reshape(
        tile_rows, tile_width // (rep_depth * block_width), rep_depth, block_width
    )
    picked = lax.dynamic_index_in_dim(shaped, rep_layer, 2, keepdims=False)
    return picked.reshape(tile_rows, tile_width // rep_depth)


def row_share(matrix, rep_depth, rep_layer, block_width):
    tile_rows, tile_width = matrix.shape
    shaped = matrix.reshape(
        tile_rows // (rep_depth * block_width), rep_depth, block_width, tile_width
    )
    picked = lax.dynamic_index_in_dim(shaped, rep_layer, 1, keepdims=False)
    return picked.reshape(tile_rows // rep_depth, tile_width)


def body(density, pattern_density, pattern_square, pattern_cube):
    tile_rows, tile_width = density.shape
    rep_depth = lax.axis_size("rep")
    rep_layer = lax.axis_index("rep")
    share_width = tile_width // rep_depth
    share_start = rep_layer * share_width
    masked = jnp.where(spread(pattern_density, BLK), density, jnp.zeros_like(density))
    right_share = row_share(masked, rep_depth, rep_layer, BLK)
    left_band = lax.all_gather(
        column_share(masked, rep_depth, rep_layer, BLK), "col", axis=1, tiled=True
    )
    right_band = lax.all_gather(right_share, "row", axis=0, tiled=True)
    product_one = jnp.dot(left_band, right_band, preferred_element_type=jnp.float32)
    square_keep = spread(pattern_square, BLK)
    summed = lax.psum(product_one, "rep")
    square = jnp.where(square_keep, summed, jnp.float32(0.0)).astype(jnp.bfloat16)
    left_square = lax.all_gather(
        column_share(square, rep_depth, rep_layer, BLK), "col", axis=1, tiled=True
    )
    product_two = jnp.dot(left_square, right_band, preferred_element_type=jnp.float32)
    cube_share = lax.psum_scatter(product_two, "rep", scatter_dimension=1, tiled=True)
    cube_keep = lax.dynamic_slice_in_dim(spread(pattern_cube, BLK), share_start, share_width, 1)
    square_cols = lax.dynamic_slice_in_dim(square, share_start, share_width, 1).astype(jnp.float32)
    cube = jnp.where(cube_keep, cube_share, jnp.float32(0.0))
    return (3.0 * square_cols - 2.0 * cube).astype(jnp.bfloat16)


def solution(mesh):
    placed = (P("row", "col"), P("row", "col"), P("row", "col"), P("row", "col"))
    return jax.shard_map(
        body, mesh=mesh, in_specs=placed, out_specs=P("row", ("col", "rep")), check_vma=False
    )
```

profile of v0, /device:TPU:1, one launch (start us, length us, event | category | flops | bytes accessed | tf_op | source)
XLA Modules:
  0.0 318.8 jit_solution(17400307454804896158)
XLA Ops:
  6.5 0.0 all-gather.4.cloned.1.call-start
  6.5 0.7 broadcast_compare_fusion.1
  7.2 3.1 broadcast_in_dim.30
  10.3 10.4 %reshape.37 = pred[512,2048]{1,0:T(8,128)(4,1)S(1)} reshape(pred[16,32,64,32]{3,2,1,0:T(8,128)(4,1)} %broadcast_in_dim.30) | data formatting | bytes 2097152 | tf_op jit(solution)/shard_map/reshape | solution.py:14
  20.7 1.8 broadcast_select_fusion
  22.5 2.5 copy.5
  25.0 0.0 copy-start
  25.0 1.9 constant_dynamic-slice_fusion.2
  26.9 0.0 all-gather.4.cloned.1.call-update
  27.0 0.0 all-gather.6.cloned.1.call-start
  27.0 0.9 constant_dynamic-slice_fusion.1
  27.9 0.0 all-gather.6.cloned.1.call-update
  27.9 0.0 all-gather.8.cloned.1.call-start
  27.9 0.0 copy-done
  28.0 3.1 broadcast_in_dim.15
  31.1 10.4 %reshape.36 = pred[512,2048]{1,0:T(8,128)(4,1)S(1)} reshape(pred[16,32,64,32]{3,2,1,0:T(8,128)(4,1)} %broadcast_in_dim.15) | data formatting | bytes 2097152 | tf_op jit(solution)/shard_map/reshape | solution.py:14
  41.4 22.9 %all-gather.4.cloned.1.call-done = bf16[512,2048]{0,1:T(8,128)(2,1)} async-done(((bf16[512,512]{0,1:T(8,128)(2,1)}), bf16[512,2048]{0,1:T(8,128)(2,1)}) %all-gather.4.cloned.1.call-update) | async-done | bytes 2097168 | tf_op jit(solution)/shard_map/all_gather | solution.py:43
  64.3 58.2 %all-gather.6.cloned.1.call-done = bf16[2048,2048]{1,0:T(8,128)(2,1)} async-done(((bf16[128,2048]{1,0:T(8,128)(2,1)}), bf16[2048,2048]{1,0:T(8,128)(2,1)}) %all-gather.6.cloned.1.call-update) | async-done | bytes 8388624 | tf_op jit(solution)/shard_map/all_gather | solution.py:46
  122.5 10.5 %fusion = f32[512,2048]{1,0:T(8,128)} fusion(bf16[512,2048]{0,1:T(8,128)(2,1)} %all-gather.4.cloned.1.call-done, bf16[2048,2048]{1,0:T(8,128)(2,1)} %all-gather.6.cloned.1.call-done), kind=kOutput, calls=%fused_computation.9 | convolution fusion | flops 4294967296 | bytes 14680064 | tf_op jit(solution)/shard_map/dot_general | solution.py:47
  133.1 78.3 %all-reduce.1 = bf16[512,2048]{1,0:T(8,128)(2,1)} all-reduce(f32[512,2048]{1,0:T(8,128)} %fusion), channel_id=1, replica_groups=mesh['row'=16,'col'=4,'rep'=4] {'rep'}, use_global_device_ids=true, to_apply=%region_0.1 | all-reduce | flops 1048576 | bytes 6291456 | tf_op jit(solution)/shard_map/psum | solution.py:49
  211.4 2.3 select_convert_fusion
  213.7 2.6 copy.6
  216.3 1.9 constant_dynamic-slice_fusion
  218.1 0.0 all-gather.8.cloned.1.call-update
  218.2 0.2 reduce-scatter.2.cloned.1.call-start
  218.4 31.4 %all-gather.8.cloned.1.call-done = bf16[512,2048]{0,1:T(8,128)(2,1)} async-done(((bf16[512,512]{0,1:T(8,128)(2,1)}), bf16[512,2048]{0,1:T(8,128)(2,1)}) %all-gather.8.cloned.1.call-update) | async-done | bytes 2097168 | tf_op jit(solution)/shard_map/all_gather | solution.py:51
  249.8 10.5 %fusion.1 = f32[512,2048]{1,0:T(8,128)} fusion(bf16[512,2048]{0,1:T(8,128)(2,1)} %all-gather.8.cloned.1.call-done, bf16[2048,2048]{1,0:T(8,128)(2,1)} %all-gather.6.cloned.1.call-done), kind=kOutput, calls=%fused_computation.10 | convolution fusion | flops 4294967296 | bytes 14680064 | tf_op jit(solution)/shard_map/dot_general | solution.py:54
  260.3 0.0 copy-start.1
  260.3 0.0 reduce-scatter.2.cloned.1.call-update
  260.3 0.7 copy-done.1
  261.0 3.1 broadcast_in_dim.33
  264.1 10.5 %reshape.42 = pred[512,2048]{1,0:T(8,128)(4,1)S(1)} reshape(pred[16,32,64,32]{3,2,1,0:T(8,128)(4,1)} %broadcast_in_dim.33) | data formatting | bytes 2097152 | tf_op jit(solution)/shard_map/reshape | solution.py:14
  274.6 35.3 %reduce-scatter.2.cloned.1.call-done = f32[512,512]{1,0:T(8,128)} async-done(((f32[512,2048]{1,0:T(8,128)}), f32[512,512]{1,0:T(8,128)}) %reduce-scatter.2.cloned.1.call-update) | async-done | bytes 1048592 | tf_op jit(solution)/shard_map/reduce_scatter | solution.py:55
  309.9 2.3 subtract_convert_fusion
  (2 shorter events, 0.0 us)
Async XLA Ops:
  6.5 57.8 %all-gather.4.cloned.1.call-start = ((), (), s32[]{:S(2)}) async-start(), calls=%async_computation.1 | async-start | bytes 2621440 | tf_op jit(solution)/shard_map/all_gather | solution.py:43
  25.0 2.9 copy-start
  27.0 95.6 %all-gather.6.cloned.1.call-start = ((), (), s32[]{:S(2)}) async-start(), calls=%async_computation.2 | async-start | bytes 8912896 | tf_op jit(solution)/shard_map/all_gather | solution.py:46
  27.9 221.9 %all-gather.8.cloned.1.call-start = ((), (), s32[]{:S(2)}) async-start(), calls=%async_computation.3 | async-start | bytes 2621440 | tf_op jit(solution)/shard_map/all_gather | solution.py:51
  218.2 91.7 %reduce-scatter.2.cloned.1.call-start = ((), (), s32[]{:S(2)}) async-start(), calls=%async_computation.4 | async-start | bytes 5242880 | tf_op jit(solution)/shard_map/reduce_scatter | solution.py:55
  260.3 0.7 copy-start.1
Sparse Core Ops, SparseCore 0:
  27.1 37.2 all-gather.3
  66.1 56.3 all-gather.5
  218.3 31.4 all-gather.7
  260.5 49.4 reduce-scatter.1
where the time goes:
time: 320 us; the launch traced here: 319 us
  waiting for transfers between devices  148 us (46%)
  blocking collectives  78.3 us (24%)
  local copies, waits for them, and re-layouts  50.9 us (16%)
  matrix products  21.1 us (7%)
  between operations  13.2 us (4%)
  other arithmetic  7.09 us (2%)
    psum x1, blocking collectives, body(): summed = lax.psum(product_one, 'rep')  78.3 us
    all_gather x1, waiting for transfers between devices, body(): right_band = lax.all_gather(right_share, 'row', axis=0, tiled=True)  58.2 us
    reduce_scatter x1, waiting for transfers between devices, body(): lax.psum_scatter(product_two, 'rep', scatter_dimension=1, tiled=True)  35.3 us
    all_gather x1, waiting for transfers between devices, body(): lax.all_gather(column_share(square, rep_depth, rep_layer, BLK), 'col', ax...  31.4 us
    reshape x3, local copies, waits for them, and re-layouts, spread(): return wide.reshape(blocks_down * block_width, blocks_across * block_width)  31.3 us
    all_gather x1, waiting for transfers between devices, body(): lax.all_gather(column_share(masked, rep_depth, rep_layer, BLK), 'col', ax...  22.9 us
    dot_general x1, matrix products, body(): jnp.dot(left_square, right_band, preferred_element_type=jnp.float32)  10.5 us
    dot_general x1, matrix products, body(): jnp.dot(left_band, right_band, preferred_element_type=jnp.float32)  10.5 us
  transfers between devices with their start and end apart: 4, of which 4 were waited for; matrix products, arithmetic and copies ran while one was open for 9% of the time, Pallas kernels for 0%

commit v1 on v0

--- a/solution.py
+++ b/solution.py
@@ -46,7 +46,7 @@
     right_band = lax.all_gather(right_share, "row", axis=0, tiled=True)
     product_one = jnp.dot(left_band, right_band, preferred_element_type=jnp.float32)
     square_keep = spread(pattern_square, BLK)
-    summed = lax.psum(product_one, "rep")
+    summed = jnp.sum(lax.all_gather(product_one, "rep"), axis=0)
     square = jnp.where(square_keep, summed, jnp.float32(0.0)).astype(jnp.bfloat16)
     left_square = lax.all_gather(
         column_share(square, rep_depth, rep_layer, BLK), "col", axis=1, tiled=True

time: 320 us -> 405 us (1.27)
  waiting for transfers between devices: 148 us -> 304 us
  blocking collectives: 78.3 us -> 0 us
  other arithmetic: 7.09 us -> 15 us
    all_gather x0 -> x1, waiting for transfers between devices: none -> 154 us  [body(): summed = jnp.sum(lax.all_gather(product_one, 'rep'), axis=0)]
    psum x1 -> x0, blocking collectives: 78.3 us -> none  [body(): summed = lax.psum(product_one, 'rep')]
    reduce_scatter x1, waiting for transfers between devices: 35.3 us -> 21.6 us  [body(): lax.psum_scatter(product_two, 'rep', scatter_dimension=1, tiled=True)]
    all_gather x1, waiting for transfers between devices: 22.9 us -> 36.4 us  [body(): lax.all_gather(column_share(masked, rep_depth, rep_layer, BLK), 'col', ax...]
    reduce_sum x0 -> x1, other arithmetic: none -> 8.11 us  [body(): summed = jnp.sum(lax.all_gather(product_one, 'rep'), axis=0)]
    broadcast_in_dim x3 -> x5, local copies, waits for them, and re-layouts: 9.28 us -> 9.8 us  [spread(): jnp.broadcast_to(pattern[:, None, :, None] > 0, (blocks_down, block_width...]
  transfers between devices with their start and end apart: 4 -> 5, of which waited for: 4 -> 5; matrix products, arithmetic and copies ran while one was open for 9% -> 7% of each run, Pallas kernels for 0% -> 0%
where the time goes in v1:
time: 405 us; the launch traced here: 404 us
  waiting for transfers between devices  304 us (75%)
  local copies, waits for them, and re-layouts  50.4 us (12%)
  matrix products  21.1 us (5%)
  other arithmetic  15 us (4%)
  between operations  13.2 us (3%)
    all_gather x1, waiting for transfers between devices, body(): summed = jnp.sum(lax.all_gather(product_one, 'rep'), axis=0)  154 us
    all_gather x1, waiting for transfers between devices, body(): right_band = lax.all_gather(right_share, 'row', axis=0, tiled=True)  58.2 us
    all_gather x1, waiting for transfers between devices, body(): lax.all_gather(column_share(masked, rep_depth, rep_layer, BLK), 'col', ax...  36.4 us
    all_gather x1, waiting for transfers between devices, body(): lax.all_gather(column_share(square, rep_depth, rep_layer, BLK), 'col', ax...  34.3 us
    reshape x3, local copies, waits for them, and re-layouts, spread(): return wide.reshape(blocks_down * block_width, blocks_across * block_width)  32 us
    reduce_scatter x1, waiting for transfers between devices, body(): lax.psum_scatter(product_two, 'rep', scatter_dimension=1, tiled=True)  21.6 us
    dot_general x1, matrix products, body(): jnp.dot(left_band, right_band, preferred_element_type=jnp.float32)  10.5 us
    dot_general x1, matrix products, body(): jnp.dot(left_square, right_band, preferred_element_type=jnp.float32)  10.5 us
  transfers between devices with their start and end apart: 5, of which 5 were waited for; matrix products, arithmetic and copies ran while one was open for 7% of the time, Pallas kernels for 0%

profile of v1, /device:TPU:1, one launch (start us, length us, event | category | flops | bytes accessed | tf_op | source)
XLA Modules:
  0.0 404.3 jit_solution(6327701106821798454)
XLA Ops:
  6.5 0.0 all-gather.6.cloned.1.call-start
  6.5 0.7 broadcast_compare_fusion.1
  7.2 3.1 broadcast_in_dim.38
  10.3 10.4 %reshape.38 = pred[512,2048]{1,0:T(8,128)(4,1)S(1)} reshape(pred[16,32,64,32]{3,2,1,0:T(8,128)(4,1)} %broadcast_in_dim.38) | data formatting | bytes 2097152 | tf_op jit(solution)/shard_map/reshape | solution.py:14
  20.7 1.8 broadcast_select_fusion
  22.5 2.5 copy.5
  25.1 1.9 constant_dynamic-slice_fusion.2
  26.9 0.0 all-gather.6.cloned.1.call-update
  27.0 0.0 all-gather.8.cloned.1.call-start
  27.0 0.8 constant_dynamic-slice_fusion.1
  27.8 0.0 all-gather.8.cloned.1.call-update
  27.9 0.0 all-gather.12.cloned.1.call-start
  27.9 36.4 %all-gather.6.cloned.1.call-done = bf16[512,2048]{0,1:T(8,128)(2,1)} async-done(((bf16[512,512]{0,1:T(8,128)(2,1)}), bf16[512,2048]{0,1:T(8,128)(2,1)}) %all-gather.6.cloned.1.call-update) | async-done | bytes 2097168 | tf_op jit(solution)/shard_map/all_gather | solution.py:43
  64.3 58.2 %all-gather.8.cloned.1.call-done = bf16[2048,2048]{1,0:T(8,128)(2,1)} async-done(((bf16[128,2048]{1,0:T(8,128)(2,1)}), bf16[2048,2048]{1,0:T(8,128)(2,1)}) %all-gather.8.cloned.1.call-update) | async-done | bytes 8388624 | tf_op jit(solution)/shard_map/all_gather | solution.py:46
  122.5 10.5 %fusion.2 = f32[512,2048]{1,0:T(8,128)} fusion(bf16[512,2048]{0,1:T(8,128)(2,1)} %all-gather.6.cloned.1.call-done, bf16[2048,2048]{1,0:T(8,128)(2,1)} %all-gather.8.cloned.1.call-done), kind=kOutput, calls=%fused_computation.12 | convolution fusion | flops 4294967296 | bytes 14680064 | tf_op jit(solution)/shard_map/dot_general | solution.py:47
  133.1 0.0 copy-start
  133.1 0.0 all-gather.12.cloned.1.call-update
  133.1 0.0 all-gather.10.cloned.1.call-start
  133.2 0.6 copy-done
  133.8 0.1 copy.6
  133.9 0.2 broadcast_in_dim.42
  134.1 0.3 broadcast_in_dim.43
  134.4 0.1 constant_dynamic-slice_fusion
  134.4 153.6 %all-gather.12.cloned.1.call-done = f32[2048,2048]{1,0:T(8,128)} async-done(((f32[512,2048]{1,0:T(8,128)}), f32[2048,2048]{1,0:T(8,128)}) %all-gather.12.cloned.1.call-update) | async-done | bytes 16777232 | tf_op jit(solution)/shard_map/all_gather | solution.py:49
  288.1 8.1 %reduce_sum.11 = bf16[512,2048]{1,0:T(8,128)(2,1)S(1)} reduce(f32[4,512,2048]{2,1,0:T(8,128)} %bitcast.19, f32[]{:T(128)} %constant.8.clone.1), dimensions={0}, to_apply=%region_0.1 | reduce | flops 3145728 | bytes 18874372 | tf_op jit(solution)/shard_map/reduce_sum | solution.py:49
  296.2 2.5 copy.7
  298.7 2.0 fusion
  300.6 0.0 all-gather.10.cloned.1.call-update
  300.7 0.2 reduce-scatter.2.cloned.1.call-start
  300.9 34.3 %all-gather.10.cloned.1.call-done = bf16[512,2048]{0,1:T(8,128)(2,1)} async-done(((bf16[512,512]{0,1:T(8,128)(2,1)}), bf16[512,2048]{0,1:T(8,128)(2,1)}) %all-gather.10.cloned.1.call-update) | async-done | bytes 2097168 | tf_op jit(solution)/shard_map/all_gather | solution.py:51
  335.2 10.5 %fusion.3 = f32[512,2048]{1,0:T(8,128)} fusion(bf16[512,2048]{0,1:T(8,128)(2,1)} %all-gather.10.cloned.1.call-done, bf16[2048,2048]{1,0:T(8,128)(2,1)} %all-gather.8.cloned.1.call-done), kind=kOutput, calls=%fused_computation.13 | convolution fusion | flops 4294967296 | bytes 14680064 | tf_op jit(solution)/shard_map/dot_general | solution.py:54
  345.8 0.0 reduce-scatter.2.cloned.1.call-update
  345.8 3.1 broadcast_in_dim.37
  348.9 0.0 copy-start.1
  348.9 10.5 %reshape.37 = pred[512,2048]{1,0:T(8,128)(4,1)S(1)} reshape(pred[16,32,64,32]{3,2,1,0:T(8,128)(4,1)} %broadcast_in_dim.37) | data formatting | bytes 2097152 | tf_op jit(solution)/shard_map/reshape | solution.py:14
  359.4 0.0 copy-done.1
  359.5 3.1 broadcast_in_dim.41
  362.6 11.2 %reshape.43 = pred[512,2048]{1,0:T(8,128)(4,1)} reshape(pred[16,32,64,32]{3,2,1,0:T(8,128)(4,1)} %broadcast_in_dim.41) | data formatting | bytes 2097152 | tf_op jit(solution)/shard_map/reshape | solution.py:14
  373.7 21.6 %reduce-scatter.2.cloned.1.call-done = f32[512,512]{1,0:T(8,128)} async-done(((f32[512,2048]{1,0:T(8,128)}), f32[512,512]{1,0:T(8,128)}) %reduce-scatter.2.cloned.1.call-update) | async-done | bytes 1048592 | tf_op jit(solution)/shard_map/reduce_scatter | solution.py:55
  395.4 2.4 subtract_convert_fusion
  (2 shorter events, 0.0 us)
Async XLA Ops:
  6.5 57.8 %all-gather.6.cloned.1.call-start = ((), (), s32[]{:S(2)}) async-start(), calls=%async_computation.1 | async-start | bytes 2621440 | tf_op jit(solution)/shard_map/all_gather | solution.py:43
  27.0 95.6 %all-gather.8.cloned.1.call-start = ((), (), s32[]{:S(2)}) async-start(), calls=%async_computation.2 | async-start | bytes 8912896 | tf_op jit(solution)/shard_map/all_gather | solution.py:46
  27.9 260.2 %all-gather.12.cloned.1.call-start = ((), (), s32[]{:S(2)}) async-start(), calls=%async_computation.5 | async-start | bytes 20971520 | tf_op jit(solution)/shard_map/all_gather | solution.py:49
  133.1 0.7 copy-start
  133.1 202.1 %all-gather.10.cloned.1.call-start = ((), (), s32[]{:S(2)}) async-start(), calls=%async_computation.3 | async-start | bytes 2621440 | tf_op jit(solution)/shard_map/all_gather | solution.py:51
  300.7 94.7 %reduce-scatter.2.cloned.1.call-start = ((), (), s32[]{:S(2)}) async-start(), calls=%async_computation.4 | async-start | bytes 5242880 | tf_op jit(solution)/shard_map/reduce_scatter | solution.py:55
  348.9 10.5 %copy-start.1 = (s32[16,64]{1,0:T(8,128)S(1)}, s32[16,64]{1,0:T(8,128)}, u32[]{:S(2)}) copy-start(s32[16,64]{1,0:T(8,128)} %param.7) | copy-start | bytes 12292
Sparse Core Ops, SparseCore 0:
  27.1 37.2 all-gather.5
  66.2 56.3 all-gather.7
  133.2 154.7 all-gather.11
  300.8 34.4 all-gather.9
  345.9 49.3 reduce-scatter.1
